TPU v7x, 32 devices: a whole 2x2x4 slice. The times are simulated.
32 devices in a mesh: slide: 2 (over x), gr: 4 (over y, core), gc: 4 (over z).
Axes of the slice: x: 2, y: 2, z: 4, core: 2. Of those that a mesh axis runs over, the one named last changes fastest.
Arguments:
- features: bfloat16 [128, 32, 512], P(('slide', 'gr'), 'gc'), parts along dimension 0, may hold values from -6 to 6
- out_grad: bfloat16 [128, 32, 512], P(('slide', 'gr'), 'gc'), parts along dimension 0, may hold values from -6 to 6
- w_in: bfloat16 [512, 1024], replicated, may hold values from -0.25 to 0.25
- w_out: bfloat16 [1024, 512], replicated, may hold values from -0.1875 to 0.1875
- decay_row: bfloat16 [128, 32, 1024], P(('slide', 'gr'), 'gc'), parts along dimension 0, may hold values from 0 to 1, as said below
- decay_col: bfloat16 [128, 32, 1024], P(('slide', 'gr'), 'gc'), parts along dimension 0, may hold values from 0 to 1, as said below
- b_proj: float32 [128, 32, 16], P(('slide', 'gr'), 'gc'), parts along dimension 0, may hold values from -6 to 6
- c_proj: float32 [128, 32, 16], P(('slide', 'gr'), 'gc'), parts along dimension 0, may hold values from -6 to 6
- tissue: int32 [128, 32], P(('slide', 'gr'), 'gc'), parts along dimension 0, may hold values from 0 to 1, as said below
Outputs:
- feat_grad: bfloat16 [128, 32, 512], P(('slide', 'gr'), 'gc'), parts along dimension 0
- w_in_grad: float32 [1024, 1024], P('slide'), parts along dimension 0
- w_out_grad: float32 [2048, 512], P('slide'), parts along dimension 0
- decay_row_grad: float32 [128, 32, 1024], P(('slide', 'gr'), 'gc'), parts along dimension 0
- decay_col_grad: float32 [128, 32, 1024], P(('slide', 'gr'), 'gc'), parts along dimension 0
- b_grad: float32 [128, 32, 16], P(('slide', 'gr'), 'gc'), parts along dimension 0
- c_grad: float32 [128, 32, 16], P(('slide', 'gr'), 'gc'), parts along dimension 0
There are 2 independent parts, one for each index of `slide`. A program takes and returns all parts, laid end to end along the dimension named above; an argument that names none is the same for every part. Nothing has to cross between parts.
Inputs may be any that keep to these rules, and one draw needn't show every extreme that they name: 1 marks a tissue tile, 0 background; the share of tissue differs from region to region of the grid. `decay_row`: decays lie in (0, 1], most close to one. `decay_col`: decays lie in (0, 1], most close to one.
All inputs are finite; a program needn't handle non-finite values.
Results may differ from a plain program's by a relative error of at most 0.011.
Values sent between devices are 32-bit elements; how exact they have to be, the bound alone decides.
A program may use at most 128 MiB of HBM per device.

v0:
```python
import math
import jax
import jax.numpy as jnp
from jax import lax
from jax.sharding import PartitionSpec as P


def prefix(part, axis, combine, identity, reverse):
    count = lax.axis_size(axis)
    place = lax.axis_index(axis)
    ahead = count - 1 - place if reverse else place
    gathered = jax.tree.map(lambda a: lax.all_gather(a, axis), part)
    state = jax.tree.map(lambda a, e: jnp.zeros_like(a) + jnp.asarray(e, a.dtype), part, identity)

    def one(turn, state):
        source = count - 1 - turn if reverse else turn
        return combine(
            state, jax.tree.map(lambda a: lax.dynamic_index_in_dim(a, source, 0, False), gathered)
        )

    return lax.fori_loop(0, ahead, one, state)


def chain_pair(earlier, later):
    return (earlier[0] * later[0], later[0][:, None, :] * earlier[1] + later[1])


def chain_identity(totals):
    return (jnp.ones_like(totals[0]), jnp.zeros_like(totals[1]))


def row_entering(totals):
    return prefix(totals, "gc", chain_pair, chain_identity(totals), False)[1]


def row_leaving(totals):
    return prefix(totals, "gc", chain_pair, chain_identity(totals), True)[1]


def block_pass(signal_blk, upstream_blk, row_decay, col_decay, b_proj, c_proj, norm_scale):
    row_count, col_count, inner = signal_blk.shape
    states_n = b_proj.shape[2]
    decay_cols = jnp.moveaxis(row_decay, 1, 0)
    signal_cols = jnp.moveaxis(signal_blk, 1, 0)
    b_cols = jnp.moveaxis(b_proj, 1, 0)

    def row_total_step(carry, inputs):
        product, state = carry
        decay_now, signal_now, b_now = inputs
        source_now = norm_scale * b_now[:, :, None] * signal_now[:, None, :]
        return ((product * decay_now, decay_now[:, None, :] * state + source_now), None)

    start_row = (
        jnp.ones((row_count, inner), jnp.float32),
        jnp.zeros((row_count, states_n, inner), jnp.float32),
    )
    row_totals, unused_row = lax.scan(row_total_step, start_row, (decay_cols, signal_cols, b_cols))
    row_in = row_entering(row_totals)

    def row_emit_step(state, inputs):
        decay_now, signal_now, b_now = inputs
        updated = (
            decay_now[:, None, :] * state + norm_scale * b_now[:, :, None] * signal_now[:, None, :]
        )
        return (updated, updated)

    unused_last, row_state_cols = lax.scan(row_emit_step, row_in, (decay_cols, signal_cols, b_cols))
    row_state = jnp.moveaxis(row_state_cols, 0, 1)

    def col_total_step(carry, inputs):
        product, state = carry
        decay_now, row_now = inputs
        return ((product * decay_now, decay_now[:, None, :] * state + row_now), None)

    start_col = (
        jnp.ones((col_count, inner), jnp.float32),
        jnp.zeros((col_count, states_n, inner), jnp.float32),
    )
    col_totals, unused_col = lax.scan(col_total_step, start_col, (col_decay, row_state))
    col_in = prefix(col_totals, "gr", chain_pair, chain_identity(col_totals), False)[1]

    def col_emit_step(state, inputs):
        decay_now, row_now, c_now, up_now = inputs
        updated = decay_now[:, None, :] * state + row_now
        mixed_now = jnp.sum(c_now[:, :, None] * updated, axis=1)
        c_now_grad = jnp.sum(up_now[:, None, :] * updated, axis=2)
        return (updated, (updated, mixed_now, c_now_grad))

    unused_top, col_outputs = lax.scan(
        col_emit_step, col_in, (col_decay, row_state, c_proj, upstream_blk)
    )
    col_state, mixed, c_part = col_outputs
    col_prev = jnp.concatenate([col_in[None], col_state[:-1]], axis=0)
    col_next = jnp.concatenate([col_decay[1:], jnp.ones_like(col_decay[:1])], axis=0)

    def col_back_total(carry, inputs):
        product, adjoint = carry
        next_now, c_now, up_now = inputs
        injected = c_now[:, :, None] * up_now[:, None, :]
        return ((product * next_now, next_now[:, None, :] * adjoint + injected), None)

    back_totals, unused_back = lax.scan(
        col_back_total, start_col, (col_next, c_proj, upstream_blk), reverse=True
    )
    col_out = (col_decay[0] * back_totals[0], col_decay[0][:, None, :] * back_totals[1])
    col_back = prefix(col_out, "gr", chain_pair, chain_identity(col_out), True)[1]

    def col_back_emit(adjoint, inputs):
        next_now, c_now, up_now, prev_now = inputs
        updated = next_now[:, None, :] * adjoint + c_now[:, :, None] * up_now[:, None, :]
        return (updated, (updated, jnp.sum(updated * prev_now, axis=1)))

    unused_first, back_outputs = lax.scan(
        col_back_emit, col_back, (col_next, c_proj, upstream_blk, col_prev), reverse=True
    )
    col_adj, col_dgrad = back_outputs
    row_next = jnp.concatenate([decay_cols[1:], jnp.ones_like(decay_cols[:1])], axis=0)
    col_adj_cols = jnp.moveaxis(col_adj, 1, 0)
    row_prev_cols = jnp.concatenate([row_in[None], row_state_cols[:-1]], axis=0)

    def row_back_total(carry, inputs):
        product, adjoint = carry
        next_now, adj_now = inputs
        return ((product * next_now, next_now[:, None, :] * adjoint + adj_now), None)

    row_back_totals, unused_rb = lax.scan(
        row_back_total, start_row, (row_next, col_adj_cols), reverse=True
    )
    row_back = row_leaving(
        (decay_cols[0] * row_back_totals[0], decay_cols[0][:, None, :] * row_back_totals[1])
    )

    def row_back_emit(adjoint, inputs):
        next_now, adj_now, prev_now, signal_now, b_now = inputs
        updated = next_now[:, None, :] * adjoint + adj_now
        dgrad_now = jnp.sum(updated * prev_now, axis=1)
        signal_now_part = norm_scale * jnp.sum(b_now[:, :, None] * updated, axis=1)
        b_now_part = norm_scale * jnp.sum(signal_now[:, None, :] * updated, axis=2)
        return (updated, (dgrad_now, signal_now_part, b_now_part))

    unused_rf, row_outputs = lax.scan(
        row_back_emit,
        row_back,
        (row_next, col_adj_cols, row_prev_cols, signal_cols, b_cols),
        reverse=True,
    )
    row_dgrad = jnp.moveaxis(row_outputs[0], 0, 1)
    signal_part = jnp.moveaxis(row_outputs[1], 0, 1)
    b_part = jnp.moveaxis(row_outputs[2], 0, 1)
    return (mixed, signal_part, row_dgrad, col_dgrad, b_part, c_part)


def shards(features, out_grad, w_in, w_out, decay_row, decay_col, b_proj, c_proj, tissue):
    row_count, col_count, model_width = features.shape
    inner = w_in.shape[1]
    grid_cells = row_count * lax.axis_size("gr") * col_count * lax.axis_size("gc")
    norm_scale = 1.0 / math.sqrt(grid_cells)
    feat_rows = features.reshape(row_count * col_count, model_width)
    grad_rows = out_grad.reshape(row_count * col_count, model_width)
    tissue_keep = tissue.astype(jnp.float32)[:, :, None]
    projected = jnp.dot(feat_rows, w_in, preferred_element_type=jnp.float32).reshape(
        row_count, col_count, inner
    )
    signal = (tissue_keep * projected).astype(jnp.bfloat16)
    upstream = lax.dot_general(
        grad_rows, w_out, (((1,), (1,)), ((), ())), preferred_element_type=jnp.float32
    )
    upstream = upstream.reshape(row_count, col_count, inner).astype(jnp.bfloat16)
    mixed_parts, signal_parts, row_parts, col_parts = ([], [], [], [])
    b_grad = jnp.zeros(b_proj.shape, jnp.float32)
    c_grad = jnp.zeros(c_proj.shape, jnp.float32)
    outcome = block_pass(
        signal.astype(jnp.float32),
        upstream.astype(jnp.float32),
        decay_row.astype(jnp.float32),
        decay_col.astype(jnp.float32),
        b_proj,
        c_proj,
        norm_scale,
    )
    mixed_parts.append(outcome[0])
    signal_parts.append(outcome[1])
    row_parts.append(outcome[2])
    col_parts.append(outcome[3])
    b_grad = b_grad + outcome[4]
    c_grad = c_grad + outcome[5]
    mixed = mixed_parts[0].astype(jnp.bfloat16)
    signal_grad = (tissue_keep * signal_parts[0]).astype(jnp.bfloat16)
    grad_flat = signal_grad.reshape(row_count * col_count, inner)
    feat_grad = lax.dot_general(
        grad_flat, w_in, (((1,), (1,)), ((), ())), preferred_element_type=jnp.float32
    )
    feat_grad = feat_grad.astype(jnp.bfloat16).reshape(row_count, col_count, model_width)
    w_in_local = lax.dot_general(
        feat_rows, grad_flat, (((0,), (0,)), ((), ())), preferred_element_type=jnp.float32
    )
    mixed_flat = mixed.reshape(row_count * col_count, inner)
    w_out_local = lax.dot_general(
        mixed_flat, grad_rows, (((0,), (0,)), ((), ())), preferred_element_type=jnp.float32
    )
    w_in_grad, w_out_grad = lax.psum((w_in_local, w_out_local), ("gr", "gc"))
    decay_row_grad = row_parts[0]
    decay_col_grad = col_parts[0]
    return (feat_grad, w_in_grad, w_out_grad, decay_row_grad, decay_col_grad, b_grad, c_grad)


def solution(mesh):
    in_specs = (
        P(("slide", "gr"), "gc", None),
        P(("slide", "gr"), "gc", None),
        P(),
        P(),
        P(("slide", "gr"), "gc", None),
        P(("slide", "gr"), "gc", None),
        P(("slide", "gr"), "gc", None),
        P(("slide", "gr"), "gc", None),
        P(("slide", "gr"), "gc"),
    )
    out_specs = (
        P(("slide", "gr"), "gc", None),
        P("slide", None),
        P("slide", None),
        P(("slide", "gr"), "gc", None),
        P(("slide", "gr"), "gc", None),
        P(("slide", "gr"), "gc", None),
        P(("slide", "gr"), "gc", None),
    )
    return jax.shard_map(shards, mesh=mesh, in_specs=in_specs, out_specs=out_specs, check_vma=False)
```

profile of v0, /device:TPU:0, one launch (start us, length us, event | category | flops | bytes accessed | tf_op | source)
XLA Modules:
  0.0 639.7 jit_solution(3221062963915205826)
XLA Ops:
  11.6 3.2 while.187
  21.0 37.7 %while.186 = (s32[]{:T(128)}, f32[8,1024]{1,0:T(8,128)S(1)}, f32[8,16,1024]{2,1,0:T(8,128)S(1)}, f32[16,8,1024]{2,1,0:T(8,128)}, f32[16,8,16]{2,1,0:T(8,128)}, /...) while((s32[]{:T(128)}, f32[8,1024]{1,0:T(8,128)S(1)}, ...), condition=%wide.region_1.2_spmd.clone, body=%wide.region_0.1_spmd.clone.sunk | while | flops 540676 | bytes 1312384 | solution.py:102
  59.7 18.5 %all-gather.2 = f32[64,1024]{1,0:T(8,128)S(1)} all-gather(f32[16,1024]{1,0:T(8,128)S(1)} %get-tuple-element.996), channel_id=4, replica_groups=mesh['slide'=2,'gr'=4,'gc'=4] {'gc'}, dimensions={0}, use_global_device_ids=true | all-gather | bytes 327680 | tf_op jit(solution)/shard_map/all_gather | solution.py:12
  78.2 25.4 %all-gather.15.cloned.1.call-done = f32[64,16,1024]{2,1,0:T(8,128)} async-done(((f32[16,16,1024]{2,1,0:T(8,128)}), f32[64,16,1024]{2,1,0:T(8,128)}) %all-gather.15.cloned.1.call-update) | async-done | bytes 4194320 | tf_op jit(solution)/shard_map/all_gather | solution.py:12
  103.8 22.9 %while.180 = (s32[]{:T(128)}, f32[16,16,1024]{2,1,0:T(8,128)S(1)}, f32[8,16,16,1024]{3,2,1,0:T(8,128)}, f32[8,16,1024]{2,1,0:T(8,128)}, f32[8,16,16]{2,1,0:T(8,128)}, /*index=5*/f32[8,16,1024]{2,1,0:T(8,128)}, s32[]{:T(128)}) while((s32[]{:T(128)}, f32[16,16,1024]{2,1,0:T(8,128)S(1)}, f32[8,16,16,1024]{3,2,1,0:T(8,128)}, ...), condition=%wide.region_9.10_spmd, body=%wide.region_8.9_spmd.sunk | while | flops 786690 | bytes 3542613 | solution.py:67
  126.7 8.4 %copy.71 = f32[8,16,16,1024]{3,2,0,1:T(8,128)} copy(f32[8,16,16,1024]{3,2,1,0:T(8,128)} %get-tuple-element.999) | data formatting | bytes 16777216 | tf_op jit(solution)/shard_map/while | solution.py:67
  135.1 33.2 %while.188 = (s32[]{:T(128)}, f32[8,1024]{1,0:T(8,128)S(1)}, f32[8,16,1024]{2,1,0:T(8,128)S(1)}, f32[16,8,1024]{2,1,0:T(8,128)}, f32[16,8,16,1024]{3,2,1,0:T(8,128)}, /*index=5*/s32[]{:T(128)}, s32[]{:T(128)}) while((s32[]{:T(128)}, f32[8,1024]{1,0:T(8,128)S(1)}, f32[8,16,1024]{2,1,0:T(8,128)S(1)}, f32[16,8,1024]{2,1,0:T(8,128)}, ...), condition=%wide.region_11.12_spmd.clone, body=%wide.region_10.11_spmd.clone.sunk | while | flops 409603 | bytes 1736800 | solution.py:79
  170.9 5.4 all-gather
  177.1 4.0 while.178
  181.2 6.1 all-gather.4
  187.3 9.1 %all-gather.17.cloned.1.call-done = f32[32,16,1024]{2,1,0:T(8,128)} async-done(((f32[8,16,1024]{2,1,0:T(8,128)}), f32[32,16,1024]{2,1,0:T(8,128)}) %all-gather.17.cloned.1.call-update) | async-done | bytes 2097168 | tf_op jit(solution)/shard_map/all_gather | solution.py:12
  198.3 79.2 %while.182 = (s32[]{:T(128)}, f32[8,16,1024]{2,1,0:T(8,128)S(1)}, f32[16,8,16,1024]{3,2,1,0:T(8,128)}, bf16[16,8,1024]{2,1,0:T(8,128)(2,1)}, f32[16,8,16]{2,1,0:...) while((s32[]{:T(128)}, f32[8,16,1024]{2,1,0:T(8,128)S(1)}, ...), condition=%wide.region_17.18_spmd, body=%wide.region_14.17_spmd.sunk | while | flops 778114 | bytes 2875505 | solution.py:89
  277.4 4.1 slice.24
  281.5 4.1 pad_maximum_fusion
  285.6 4.3 broadcast.84.clone
  290.0 57.4 %while.183 = (s32[]{:T(128)}, f32[8,16,1024]{2,1,0:T(8,128)S(1)}, f32[16,8,16,1024]{3,2,0,1:T(8,128)}, f32[16,8,1024]{2,1,0:T(8,128)S(1)}, f32[16,8,1024]{2,1,0:...) while((s32[]{:T(128)}, f32[8,16,1024]{2,1,0:T(8,128)S(1)}, ...), condition=%wide.region_20.21_spmd, body=%wide.region_18.20_spmd.sunk | while | flops 647171 | bytes 2918021 | solution.py:113
  348.2 29.1 %while.189 = (s32[]{:T(128)}, f32[16,1024]{1,0:T(8,128)S(1)}, f32[16,16,1024]{2,1,0:T(8,128)}, f32[8,16,1024]{2,1,0:T(8,128)}, f32[8,16,16,1024]{3,2,1,0:T(8,128)}, /*index=5*/s32[]{:T(128)}, s32[]{:T(128)}, s32[]{:T(128)}) while((s32[]{:T(128)}, f32[16,1024]{1,0:T(8,128)S(1)}, f32[16,16,1024]{2,1,0:T(8,128)}, ...), condition=%wide.region_22.23_spmd.clone, body=%wide.region_21.22_spmd.clone.sunk | while | flops 819204 | bytes 3473524 | solution.py:126
  352.4 2.8 bitcast_add_fusion.21
  356.1 2.8 bitcast_add_fusion.21
  359.8 2.8 bitcast_add_fusion.21
  363.5 2.8 bitcast_add_fusion.21
  367.1 2.8 bitcast_add_fusion.21
  374.5 2.8 bitcast_add_fusion.21
  379.8 3.8 slice.25
  383.6 4.2 pad_maximum_fusion.1
  388.6 16.8 %all-gather.6 = f32[64,1024]{1,0:T(8,128)S(1)} all-gather(f32[16,1024]{1,0:T(8,128)S(1)} %fusion.17), channel_id=8, replica_groups=mesh['slide'=2,'gr'=4,'gc'=4] {'gc'}, dimensions={0}, use_global_device_ids=true | all-gather | bytes 327680 | tf_op jit(solution)/shard_map/all_gather | solution.py:12
  407.3 60.0 %all-gather.19.cloned.1.call-done = f32[64,16,1024]{2,1,0:T(8,128)} async-done(((f32[16,16,1024]{2,1,0:T(8,128)}), f32[64,16,1024]{2,1,0:T(8,128)}) %all-gather.19.cloned.1.call-update) | async-done | bytes 4194320 | tf_op jit(solution)/shard_map/all_gather | solution.py:12
  467.3 5.5 while.184
  473.0 40.8 %while.185 = (s32[]{:T(128)}, f32[16,16,1024]{2,1,0:T(8,128)S(1)}, f32[8,16,1024]{2,0,1:T(8,128)S(1)}, f32[8,16,1024]{2,0,1:T(8,128)S(1)}, f32[8,16,16]{2,0,1:T(...) while((s32[]{:T(128)}, f32[16,16,1024]{2,1,0:T(8,128)S(1)}, ...), condition=%wide.region_29.30_spmd, body=%wide.region_25.29_spmd.sunk | while | flops 2080771 | bytes 5382305 | solution.py:141
  516.8 110.4 %all-reduce.5.cloned.1.call-done = (f32[512,1024]{0,1:T(8,128)}, f32[1024,512]{1,0:T(8,128)}) async-done(((f32[512,1024]{0,1:T(8,128)}, f32[1024,512]{1,0:T(8,128)}), (f32[512,1024]{0,1:T(8,128)}, f32[1024,512]{1,0:T(8,128)})) %all-reduce.5.cloned.1.call-update) | async-done | bytes 4194320 | tf_op jit(solution)/shard_map/psum | solution.py:201
  627.2 2.9 copy.59
  630.1 3.1 copy.199
  (521 shorter events, 319.8 us)
Async XLA Ops:
  7.2 2.0 copy-start
  7.2 96.4 %all-gather.15.cloned.1.call-start = ((), (), s32[]{:S(2)}) async-start(), calls=%async_computation.1 | async-start | bytes 5242880 | tf_op jit(solution)/shard_map/all_gather | solution.py:12
  9.2 6.7 %copy-start.9 = (bf16[16,8,1024]{2,1,0:T(8,128)(2,1)S(1)}, bf16[16,8,1024]{2,1,0:T(8,128)(2,1)}, u32[]{:S(2)}) copy-start(bf16[16,8,1024]{2,1,0:T(8,128)(2,1)} %param.38) | copy-start | bytes 786436
  14.8 1.0 copy-start.1
  14.8 1.9 copy-start.10
  14.9 88.8 %copy-start.6 = (f32[8,16,1024]{2,1,0:T(8,128)}, f32[8,16,1024]{2,1,0:T(8,128)S(1)}, u32[]{:S(2)}) copy-start(f32[8,16,1024]{2,1,0:T(8,128)S(1)} %get-tuple-element.2221) | copy-start | bytes 1572868
  14.9 88.8 %copy-start.8 = (f32[8,16,1024]{2,1,0:T(8,128)}, f32[8,16,1024]{2,1,0:T(8,128)S(1)}, u32[]{:S(2)}) copy-start(f32[8,16,1024]{2,1,0:T(8,128)S(1)} %get-tuple-element.2223) | copy-start | bytes 1572868
  15.8 161.2 %all-gather.13.cloned.1.call-start = ((), (), s32[]{:S(2)}) async-start(), calls=%async_computation | async-start | bytes 2621440 | tf_op jit(solution)/shard_map/all_gather | solution.py:12
  59.6 136.7 %all-gather.17.cloned.1.call-start = ((), (), s32[]{:S(2)}) async-start(), calls=%async_computation.2 | async-start | bytes 2621440 | tf_op jit(solution)/shard_map/all_gather | solution.py:12
  126.7 8.4 %copy-start.4 = (f32[8,16,1024]{2,1,0:T(8,128)S(1)}, f32[8,16,1024]{2,1,0:T(8,128)}, u32[]{:S(2)}) copy-start(f32[8,16,1024]{2,1,0:T(8,128)} %custom-call.5) | copy-start | bytes 1572868
  135.1 34.1 %copy-start.7 = (f32[8,16,1024]{2,1,0:T(8,128)S(1)}, f32[8,16,1024]{2,1,0:T(8,128)}, u32[]{:S(2)}) copy-start(f32[8,16,1024]{2,1,0:T(8,128)} %get-tuple-element.2222) | copy-start | bytes 1572868
  168.3 0.8 copy-start.5
  169.2 298.1 %all-gather.19.cloned.1.call-start = ((), (), s32[]{:S(2)}) async-start(), calls=%async_computation.3 | async-start | bytes 5242880 | tf_op jit(solution)/shard_map/all_gather | solution.py:12
  196.4 0.8 copy-start.2
  277.4 4.1 copy-start.3
  347.4 0.8 copy-start.12
  379.6 247.6 %all-reduce.5.cloned.1.call-start = ((), (), s32[]{:S(2)}) async-start(), calls=%async_computation.4 | async-start | bytes 8388608 | tf_op jit(solution)/shard_map/psum | solution.py:201
  383.6 21.9 %copy-start.13 = (bf16[16,8,1024]{2,1,0:T(8,128)(2,1)S(1)}, bf16[16,8,1024]{2,1,0:T(8,128)(2,1)}, u32[]{:S(2)}) copy-start(bf16[16,8,1024]{2,1,0:T(8,128)(2,1)} %get-tuple-element.1009) | copy-start | bytes 786436
  383.6 21.9 %copy-start.14 = (bf16[16,8,512]{2,1,0:T(8,128)(2,1)S(1)}, bf16[16,8,512]{2,1,0:T(8,128)(2,1)}, u32[]{:S(2)}) copy-start(bf16[16,8,512]{2,1,0:T(8,128)(2,1)} %param.34) | copy-start | bytes 393220
  472.9 40.8 %copy-start.15 = (bf16[16,8,512]{2,1,0:T(8,128)(2,1)S(1)}, bf16[16,8,512]{2,1,0:T(8,128)(2,1)}, u32[]{:S(2)}) copy-start(bf16[16,8,512]{2,1,0:T(8,128)(2,1)} %param.33) | copy-start | bytes 393220
  513.7 1.9 copy-start.11
  513.8 1.9 copy-start.16
Sparse Core Ops, SparseCore 0:
  15.9 87.5 all-gather.14
  105.1 21.1 all-gather.12
  169.3 26.9 all-gather.16
  379.8 87.4 all-gather.18
  515.8 111.3 all-reduce.4
where the time goes:
time: 652 us; the launch traced here: 640 us
  waiting for transfers between devices  205 us (31%)
  other arithmetic  182 us (28%)
  local copies, waits for them, and re-layouts  181 us (28%)
  blocking collectives  46.9 us (7%)
  between operations  14.2 us (2%)
  matrix products  8.64 us (1%)
    psum x1, waiting for transfers between devices, shards(): w_in_grad, w_out_grad = lax.psum((w_in_local, w_out_local), ('gr', 'gc'))  110 us
    all_gather x4, waiting for transfers between devices, prefix(): gathered = jax.tree.map(lambda a: lax.all_gather(a, axis), part)  94.4 us
    all_gather x4, blocking collectives, prefix(): gathered = jax.tree.map(lambda a: lax.all_gather(a, axis), part)  46.9 us
    dynamic_update_slice x80, local copies, waits for them, and re-layouts, block_pass(): lax.scan(col_emit_step, col_in, (col_decay, row_state, c_proj, upstream_b...  46.4 us
    mul x32, local copies, waits for them, and re-layouts, col_back_emit(): c_now[:, :, None] * up_now[:, None, :]  23.5 us
    mul x32, local copies, waits for them, and re-layouts, col_back_total(): injected = c_now[:, :, None] * up_now[:, None, :]  23.2 us
    reduce_sum x16, other arithmetic, col_emit_step(): c_now_grad = jnp.sum(up_now[:, None, :] * updated, axis=2)  22.9 us
    add x8, other arithmetic, row_back_total(): next_now[:, None, :] * adjoint + adj_now  22.2 us
  transfers between devices with their start and end apart: 5, of which 4 were waited for; matrix products, arithmetic and copies ran while one was open for 20% of the time, Pallas kernels for 0%

commit v1 on v0

--- a/solution.py
+++ b/solution.py
@@ -3,6 +3,11 @@
 import jax.numpy as jnp
 from jax import lax
 from jax.sharding import PartitionSpec as P
+
+
+def one_after_other(array, axis_one, axis_two):
+    half = lax.psum(array, axis_one)
+    return lax.psum(half, axis_two)
 
 
 def prefix(part, axis, combine, identity, reverse):
@@ -198,7 +203,7 @@
     w_out_local = lax.dot_general(
         mixed_flat, grad_rows, (((0,), (0,)), ((), ())), preferred_element_type=jnp.float32
     )
-    w_in_grad, w_out_grad = lax.psum((w_in_local, w_out_local), ("gr", "gc"))
+    w_in_grad, w_out_grad = one_after_other((w_in_local, w_out_local), "gc", "gr")
     decay_row_grad = row_parts[0]
     decay_col_grad = col_parts[0]
     return (feat_grad, w_in_grad, w_out_grad, decay_row_grad, decay_col_grad, b_grad, c_grad)

time: 652 us -> 783 us (1.20)
  waiting for transfers between devices: 205 us -> 335 us
    psum x1 -> x2, waiting for transfers between devices: 110 us -> 241 us  [the longest x1 155 us: one_after_other(): half = lax.psum(array, axis_one)]
  transfers between devices with their start and end apart: 5 -> 6, of which waited for: 4 -> 5; matrix products, arithmetic and copies ran while one was open for 20% -> 16% of each run, Pallas kernels for 0% -> 0%
where the time goes in v1:
time: 783 us; the launch traced here: 771 us
  waiting for transfers between devices  335 us (43%)
  other arithmetic  182 us (23%)
  local copies, waits for them, and re-layouts  180 us (23%)
  blocking collectives  46.9 us (6%)
  between operations  14.6 us (2%)
  matrix products  8.65 us (1%)
    psum x1, waiting for transfers between devices, one_after_other(): half = lax.psum(array, axis_one)  155 us
    all_gather x4, waiting for transfers between devices, prefix(): gathered = jax.tree.map(lambda a: lax.all_gather(a, axis), part)  94.4 us
    psum x1, waiting for transfers between devices, one_after_other(): return lax.psum(half, axis_two)  86 us
    all_gather x4, blocking collectives, prefix(): gathered = jax.tree.map(lambda a: lax.all_gather(a, axis), part)  46.9 us
    dynamic_update_slice x80, local copies, waits for them, and re-layouts, block_pass(): lax.scan(col_emit_step, col_in, (col_decay, row_state, c_proj, upstream_b...  46.2 us
    mul x32, local copies, waits for them, and re-layouts, col_back_emit(): c_now[:, :, None] * up_now[:, None, :]  23.5 us
    mul x32, local copies, waits for them, and re-layouts, col_back_total(): injected = c_now[:, :, None] * up_now[:, None, :]  23.2 us
    reduce_sum x16, other arithmetic, col_emit_step(): c_now_grad = jnp.sum(up_now[:, None, :] * updated, axis=2)  22.9 us
  transfers between devices with their start and end apart: 6, of which 5 were waited for; matrix products, arithmetic and copies ran while one was open for 16% of the time, Pallas kernels for 0%

profile of v1, /device:TPU:0, one launch (start us, length us, event | category | flops | bytes accessed | tf_op | source)
XLA Modules:
  0.0 770.5 jit_solution(11087940449891722671)
XLA Ops:
  11.6 3.2 while.187
  21.0 37.7 %while.186 = (s32[]{:T(128)}, f32[8,1024]{1,0:T(8,128)S(1)}, f32[8,16,1024]{2,1,0:T(8,128)S(1)}, f32[16,8,1024]{2,1,0:T(8,128)}, f32[16,8,16]{2,1,0:T(8,128)}, /...) while((s32[]{:T(128)}, f32[8,1024]{1,0:T(8,128)S(1)}, ...), condition=%wide.region_1.2_spmd.clone, body=%wide.region_0.1_spmd.clone.sunk | while | flops 540676 | bytes 1312384 | solution.py:107
  59.6 18.6 %all-gather.2 = f32[64,1024]{1,0:T(8,128)S(1)} all-gather(f32[16,1024]{1,0:T(8,128)S(1)} %get-tuple-element.996), channel_id=4, replica_groups=mesh['slide'=2,'gr'=4,'gc'=4] {'gc'}, dimensions={0}, use_global_device_ids=true | all-gather | bytes 327680 | tf_op jit(solution)/shard_map/all_gather | solution.py:17
  78.2 25.4 %all-gather.15.cloned.1.call-done = f32[64,16,1024]{2,1,0:T(8,128)} async-done(((f32[16,16,1024]{2,1,0:T(8,128)}), f32[64,16,1024]{2,1,0:T(8,128)}) %all-gather.15.cloned.1.call-update) | async-done | bytes 4194320 | tf_op jit(solution)/shard_map/all_gather | solution.py:17
  103.8 23.0 %while.180 = (s32[]{:T(128)}, f32[16,16,1024]{2,1,0:T(8,128)S(1)}, f32[8,16,16,1024]{3,2,1,0:T(8,128)}, f32[8,16,1024]{2,1,0:T(8,128)}, f32[8,16,16]{2,1,0:T(8,128)}, /*index=5*/f32[8,16,1024]{2,1,0:T(8,128)}, s32[]{:T(128)}) while((s32[]{:T(128)}, f32[16,16,1024]{2,1,0:T(8,128)S(1)}, f32[8,16,16,1024]{3,2,1,0:T(8,128)}, ...), condition=%wide.region_9.10_spmd, body=%wide.region_8.9_spmd.sunk | while | flops 786690 | bytes 3542613 | solution.py:72
  126.8 8.4 %copy.71 = f32[8,16,16,1024]{3,2,0,1:T(8,128)} copy(f32[8,16,16,1024]{3,2,1,0:T(8,128)} %get-tuple-element.999) | data formatting | bytes 16777216 | tf_op jit(solution)/shard_map/while | solution.py:72
  135.2 33.2 %while.188 = (s32[]{:T(128)}, f32[8,1024]{1,0:T(8,128)S(1)}, f32[8,16,1024]{2,1,0:T(8,128)S(1)}, f32[16,8,1024]{2,1,0:T(8,128)}, f32[16,8,16,1024]{3,2,1,0:T(8,128)}, /*index=5*/s32[]{:T(128)}, s32[]{:T(128)}) while((s32[]{:T(128)}, f32[8,1024]{1,0:T(8,128)S(1)}, f32[8,16,1024]{2,1,0:T(8,128)S(1)}, f32[16,8,1024]{2,1,0:T(8,128)}, ...), condition=%wide.region_11.12_spmd.clone, body=%wide.region_10.11_spmd.clone.sunk | while | flops 409603 | bytes 1736800 | solution.py:84
  170.9 5.4 all-gather
  177.2 4.0 while.178
  181.2 6.1 all-gather.4
  187.3 9.0 %all-gather.17.cloned.1.call-done = f32[32,16,1024]{2,1,0:T(8,128)} async-done(((f32[8,16,1024]{2,1,0:T(8,128)}), f32[32,16,1024]{2,1,0:T(8,128)}) %all-gather.17.cloned.1.call-update) | async-done | bytes 2097168 | tf_op jit(solution)/shard_map/all_gather | solution.py:17
  198.3 79.2 %while.182 = (s32[]{:T(128)}, f32[8,16,1024]{2,1,0:T(8,128)S(1)}, f32[16,8,16,1024]{3,2,1,0:T(8,128)}, bf16[16,8,1024]{2,1,0:T(8,128)(2,1)}, f32[16,8,16]{2,1,0:...) while((s32[]{:T(128)}, f32[8,16,1024]{2,1,0:T(8,128)S(1)}, ...), condition=%wide.region_17.18_spmd, body=%wide.region_14.17_spmd.sunk | while | flops 778114 | bytes 2875505 | solution.py:94
  277.5 4.1 slice.24
  281.6 4.1 pad_maximum_fusion
  285.7 4.3 broadcast.84.clone
  290.0 57.3 %while.183 = (s32[]{:T(128)}, f32[8,16,1024]{2,1,0:T(8,128)S(1)}, f32[16,8,16,1024]{3,2,0,1:T(8,128)}, f32[16,8,1024]{2,1,0:T(8,128)S(1)}, f32[16,8,1024]{2,1,0:...) while((s32[]{:T(128)}, f32[8,16,1024]{2,1,0:T(8,128)S(1)}, ...), condition=%wide.region_20.21_spmd, body=%wide.region_18.20_spmd.sunk | while | flops 647171 | bytes 2918021 | solution.py:118
  348.1 29.1 %while.189 = (s32[]{:T(128)}, f32[16,1024]{1,0:T(8,128)S(1)}, f32[16,16,1024]{2,1,0:T(8,128)}, f32[8,16,1024]{2,1,0:T(8,128)}, f32[8,16,16,1024]{3,2,1,0:T(8,128)}, /*index=5*/s32[]{:T(128)}, s32[]{:T(128)}, s32[]{:T(128)}) while((s32[]{:T(128)}, f32[16,1024]{1,0:T(8,128)S(1)}, f32[16,16,1024]{2,1,0:T(8,128)}, ...), condition=%wide.region_22.23_spmd.clone, body=%wide.region_21.22_spmd.clone.sunk | while | flops 819204 | bytes 3473524 | solution.py:131
  352.3 2.8 bitcast_add_fusion.21
  356.0 2.8 bitcast_add_fusion.21
  359.7 2.8 bitcast_add_fusion.21
  363.3 2.8 bitcast_add_fusion.21
  370.7 2.8 bitcast_add_fusion.21
  379.6 3.8 slice.25
  383.5 4.2 pad_maximum_fusion.1
  388.5 16.8 %all-gather.6 = f32[64,1024]{1,0:T(8,128)S(1)} all-gather(f32[16,1024]{1,0:T(8,128)S(1)} %fusion.17), channel_id=8, replica_groups=mesh['slide'=2,'gr'=4,'gc'=4] {'gc'}, dimensions={0}, use_global_device_ids=true | all-gather | bytes 327680 | tf_op jit(solution)/shard_map/all_gather | solution.py:17
  407.1 59.9 %all-gather.19.cloned.1.call-done = f32[64,16,1024]{2,1,0:T(8,128)} async-done(((f32[16,16,1024]{2,1,0:T(8,128)}), f32[64,16,1024]{2,1,0:T(8,128)}) %all-gather.19.cloned.1.call-update) | async-done | bytes 4194320 | tf_op jit(solution)/shard_map/all_gather | solution.py:17
  467.2 5.5 while.184
  472.8 40.8 %while.185 = (s32[]{:T(128)}, f32[16,16,1024]{2,1,0:T(8,128)S(1)}, f32[8,16,1024]{2,0,1:T(8,128)S(1)}, f32[8,16,1024]{2,0,1:T(8,128)S(1)}, f32[8,16,16]{2,0,1:T(...) while((s32[]{:T(128)}, f32[16,16,1024]{2,1,0:T(8,128)S(1)}, ...), condition=%wide.region_29.30_spmd, body=%wide.region_25.29_spmd.sunk | while | flops 2080771 | bytes 5382305 | solution.py:146
  515.6 154.9 %all-reduce.7.cloned.1.call-done = (f32[512,1024]{0,1:T(8,128)}, f32[1024,512]{1,0:T(8,128)}) async-done(((f32[512,1024]{0,1:T(8,128)}, f32[1024,512]{1,0:T(8,128)}), (f32[512,1024]{0,1:T(8,128)}, f32[1024,512]{1,0:T(8,128)})) %all-reduce.7.cloned.1.call-update) | async-done | bytes 4194320 | tf_op jit(solution)/shard_map/psum | solution.py:9
  671.7 86.0 %all-reduce.9.cloned.1.call-done = (f32[512,1024]{0,1:T(8,128)}, f32[1024,512]{1,0:T(8,128)}) async-done(((f32[512,1024]{0,1:T(8,128)}, f32[1024,512]{1,0:T(8,128)}), (f32[512,1024]{0,1:T(8,128)}, f32[1024,512]{1,0:T(8,128)})) %all-reduce.9.cloned.1.call-update) | async-done | bytes 4194320 | tf_op jit(solution)/shard_map/psum | solution.py:10
  757.7 2.9 copy.59
  760.6 3.1 copy.201
  (524 shorter events, 322.5 us)
Async XLA Ops:
  7.2 2.0 copy-start
  7.2 96.4 %all-gather.15.cloned.1.call-start = ((), (), s32[]{:S(2)}) async-start(), calls=%async_computation.1 | async-start | bytes 5242880 | tf_op jit(solution)/shard_map/all_gather | solution.py:17
  9.2 6.7 copy-start.9
  14.8 1.0 copy-start.1
  14.8 1.9 copy-start.10
  14.9 88.8 %copy-start.6 = (f32[8,16,1024]{2,1,0:T(8,128)}, f32[8,16,1024]{2,1,0:T(8,128)S(1)}, u32[]{:S(2)}) copy-start(f32[8,16,1024]{2,1,0:T(8,128)S(1)} %get-tuple-element.2227) | copy-start | bytes 1572868
  14.9 88.8 %copy-start.8 = (f32[8,16,1024]{2,1,0:T(8,128)}, f32[8,16,1024]{2,1,0:T(8,128)S(1)}, u32[]{:S(2)}) copy-start(f32[8,16,1024]{2,1,0:T(8,128)S(1)} %get-tuple-element.2229) | copy-start | bytes 1572868
  15.8 161.3 %all-gather.13.cloned.1.call-start = ((), (), s32[]{:S(2)}) async-start(), calls=%async_computation | async-start | bytes 2621440 | tf_op jit(solution)/shard_map/all_gather | solution.py:17
  59.6 136.8 %all-gather.17.cloned.1.call-start = ((), (), s32[]{:S(2)}) async-start(), calls=%async_computation.2 | async-start | bytes 2621440 | tf_op jit(solution)/shard_map/all_gather | solution.py:17
  126.8 8.4 %copy-start.4 = (f32[8,16,1024]{2,1,0:T(8,128)S(1)}, f32[8,16,1024]{2,1,0:T(8,128)}, u32[]{:S(2)}) copy-start(f32[8,16,1024]{2,1,0:T(8,128)} %custom-call.5) | copy-start | bytes 1572868
  135.2 34.1 %copy-start.7 = (f32[8,16,1024]{2,1,0:T(8,128)S(1)}, f32[8,16,1024]{2,1,0:T(8,128)}, u32[]{:S(2)}) copy-start(f32[8,16,1024]{2,1,0:T(8,128)} %get-tuple-element.2228) | copy-start | bytes 1572868
  168.4 0.8 copy-start.5
  169.2 297.9 %all-gather.19.cloned.1.call-start = ((), (), s32[]{:S(2)}) async-start(), calls=%async_computation.3 | async-start | bytes 5242880 | tf_op jit(solution)/shard_map/all_gather | solution.py:17
  196.4 0.9 copy-start.2
  277.5 4.1 copy-start.3
  347.3 0.8 copy-start.12
  379.5 291.0 %all-reduce.7.cloned.1.call-start = ((), (), s32[]{:S(2)}) async-start(), calls=%async_computation.4 | async-start | bytes 8388608 | tf_op jit(solution)/shard_map/psum | solution.py:9
  383.4 21.9 %copy-start.13 = (bf16[16,8,1024]{2,1,0:T(8,128)(2,1)S(1)}, bf16[16,8,1024]{2,1,0:T(8,128)(2,1)}, u32[]{:S(2)}) copy-start(bf16[16,8,1024]{2,1,0:T(8,128)(2,1)} %get-tuple-element.1009) | copy-start | bytes 786436
  383.4 21.9 %copy-start.14 = (bf16[16,8,512]{2,1,0:T(8,128)(2,1)S(1)}, bf16[16,8,512]{2,1,0:T(8,128)(2,1)}, u32[]{:S(2)}) copy-start(bf16[16,8,512]{2,1,0:T(8,128)(2,1)} %param.34) | copy-start | bytes 393220
  472.8 40.8 %copy-start.15 = (bf16[16,8,512]{2,1,0:T(8,128)(2,1)S(1)}, bf16[16,8,512]{2,1,0:T(8,128)(2,1)}, u32[]{:S(2)}) copy-start(bf16[16,8,512]{2,1,0:T(8,128)(2,1)} %param.33) | copy-start | bytes 393220
  513.6 1.9 copy-start.11
  513.6 1.9 copy-start.16
  515.6 242.2 %all-reduce.9.cloned.1.call-start = ((), (), s32[]{:S(2)}) async-start(), calls=%async_computation.5 | async-start | bytes 8388608 | tf_op jit(solution)/shard_map/psum | solution.py:10
Sparse Core Ops, SparseCore 0:
  15.9 87.5 all-gather.14
  105.1 21.1 all-gather.12
  169.3 26.9 all-gather.16
  379.6 87.4 all-gather.18
  515.7 154.8 all-reduce.6
  673.0 84.6 all-reduce.8
